TPU v7x, 512 devices: a whole 4x8x8 slice. The times are simulated.
512 devices in a mesh: sx: 8 (over y), sy: 16 (over x, z_lo, core), blk: 4 (over z_hi).
Axes of the slice: x: 4, y: 8, z: 8 (z_hi: 4, z_lo: 2; z = z_hi * 2 + z_lo), core: 2. Of those that a mesh axis runs over, the one named last changes fastest.
Arguments:
- snapshots: bfloat16 [4, 320, 262144], P('blk', None, ('sx', 'sy')), may hold values from -6 to 6
- offsets: int32 [4], P('blk'), may hold values from 0 to 64
- freqs: int32 [64], replicated, may hold values from 1 to 127, as said below
- modes: bfloat16 [64, 2, 8, 262144], P('blk', None, None, ('sx', 'sy')), may hold values from -6 to 6
- cell_weights: float32 [262144], P(('sx', 'sy')), may hold values from 0.5 to 2
- filter_weights: float32 [64, 8], P('blk'), may hold values from 0.05 to 1
Outputs:
- filtered: bfloat16 [4, 256, 262144], P('blk', None, ('sx', 'sy'))
Inputs may be any that keep to these rules, and one draw needn't show every extreme that they name: `freqs`: distinct values; both 1 and 127 appear.
All inputs are finite; a program needn't handle non-finite values.
Results may differ from a plain program's by a relative error of at most 0.018.
Values may be sent and summed in bfloat16 or wider, within the bound.
A program may use at most 64 MiB of HBM per device.

v0:
```python
import math

import jax
import jax.numpy as jnp
from jax import lax
from jax.sharding import PartitionSpec as P

NFFT = 256
NF = 64


def dft_tables(freqs, length):
    times = jnp.arange(length, dtype=jnp.int32)
    phase = freqs[:, None] * times[None, :] % length
    angle = phase.astype(jnp.float32) * (2.0 * math.pi / length)
    stacked = jnp.stack([jnp.cos(angle), -jnp.sin(angle)], axis=1).reshape(
        2 * freqs.shape[0], length
    )
    forward = (stacked / math.sqrt(length)).astype(jnp.bfloat16)
    inverse = (stacked.T / math.sqrt(freqs.shape[0])).astype(jnp.bfloat16)
    return (forward, inverse)


def project_filter(spectra, mode_block, cell_weights, gains):
    weighted = (spectra.astype(jnp.float32) * cell_weights).astype(jnp.bfloat16)
    product = jnp.einsum(
        "bfrc,fskc->bfrsk", weighted, mode_block, preferred_element_type=jnp.float32
    )
    part_real = product[:, :, 0, 0] + product[:, :, 1, 1]
    part_imag = product[:, :, 1, 0] - product[:, :, 0, 1]
    local_sums = jnp.stack([part_real, part_imag], axis=2)
    scale_factor = 1.0 / math.sqrt(cell_weights.shape[0] * lax.axis_size(("sx", "sy")))
    gain_table = jnp.broadcast_to(gains[None, :, None, :], local_sums.shape)
    summed = lax.psum(local_sums, ("sx", "sy"))
    scaled = gain_table * (summed * scale_factor)
    scaled = scaled.astype(jnp.bfloat16)
    scaled_real = scaled[:, :, 0]
    scaled_imag = scaled[:, :, 1]
    modes_real = mode_block[:, 0]
    modes_imag = mode_block[:, 1]
    rebuilt_real = jnp.einsum(
        "fkc,bfk->bfc", modes_real, scaled_real, preferred_element_type=jnp.float32
    ) - jnp.einsum("fkc,bfk->bfc", modes_imag, scaled_imag, preferred_element_type=jnp.float32)
    rebuilt_imag = jnp.einsum(
        "fkc,bfk->bfc", modes_real, scaled_imag, preferred_element_type=jnp.float32
    ) + jnp.einsum("fkc,bfk->bfc", modes_imag, scaled_real, preferred_element_type=jnp.float32)
    return jnp.stack([rebuilt_real, rebuilt_imag], axis=2).astype(jnp.bfloat16)


def per_device(snapshots, offsets, freqs, modes, cell_weights, filter_weights):
    forward, inverse = dft_tables(freqs, NFFT)
    cell_count = snapshots.shape[2]
    window = lax.dynamic_slice_in_dim(snapshots[0], offsets[0], NFFT, 0)
    spectra = jnp.dot(forward, window, preferred_element_type=jnp.float32).astype(jnp.bfloat16)
    spectra = spectra.reshape(1, NF, 2, cell_count)
    grouped = lax.all_to_all(spectra, "blk", split_axis=1, concat_axis=0, tiled=True)
    rebuilt = project_filter(grouped, modes, cell_weights, filter_weights)
    returned = lax.all_to_all(rebuilt, "blk", split_axis=0, concat_axis=1, tiled=True)
    flat_block = returned.reshape(2 * NF, cell_count)
    result = jnp.dot(inverse, flat_block, preferred_element_type=jnp.float32).astype(jnp.bfloat16)
    return result[None]


def solution(mesh):
    placed = (
        P("blk", None, ("sx", "sy")),
        P("blk"),
        P(),
        P("blk", None, None, ("sx", "sy")),
        P(("sx", "sy")),
        P("blk", None),
    )
    return jax.shard_map(
        per_device,
        mesh=mesh,
        in_specs=placed,
        out_specs=P("blk", None, ("sx", "sy")),
        check_vma=False,
    )
```

profile of v0, /device:TPU:1, one launch (start us, length us, event | category | flops | bytes accessed | tf_op | source)
XLA Modules:
  0.0 601.3 jit_solution(5333261102815545733)
XLA Ops:
  0.0 0.0 copy-start
  0.8 1.0 fusion.30
  1.8 0.1 copy.41
  1.9 0.0 copy-done
  1.9 0.5 convolution_convert_fusion.1
  2.4 0.0 copy-start.3
  2.4 1.1 reshape.159
  3.5 0.0 copy-start.2
  3.5 11.0 %all-to-all-start = ((bf16[1,64,2,2048]{3,2,0,1:T(2,128)(2,1)}), bf16[1,64,2,2048]{3,2,0,1:T(2,128)(2,1)S(1)}, u32[]{:S(2)}, u32[]{:S(2)}) async-start(bf16[1,64,2,2048]{3,2,0,1:T(2,128)(2,1)} %bitcast.2), calls=%async_computation | async-start | bytes 1048576 | tf_op jit(solution)/shard_map/all_to_all | solution.py:56
  14.5 0.0 copy-done.3
  14.5 0.0 copy-start.1
  14.5 0.1 copy.47
  14.6 11.8 %all-to-all-done = bf16[1,64,2,2048]{3,2,0,1:T(2,128)(2,1)S(1)} async-done(((bf16[1,64,2,2048]{3,2,0,1:T(2,128)(2,1)}), bf16[1,64,2,2048]{3,2,0,1:T(2,128)(2,1)S(1)}, u32[]{:S(2)}, u32[]{:S(2)}) %all-to-all-start) | async-done | bytes 524320 | tf_op jit(solution)/shard_map/all_to_all | solution.py:56
  26.4 0.2 copy.43
  26.6 0.0 copy-done.2
  26.6 0.1 fusion.9
  26.7 0.0 copy-done.1
  26.7 2.5 convolution_bitcast_fusion
  29.3 553.0 %psum.7 = f32[4,16,2,8]{3,0,1,2:T(4,128)S(1)} all-reduce(f32[4,16,2,8]{3,0,1,2:T(4,128)S(1)} %pad_maximum_fusion.2), channel_id=1, replica_groups=mesh['sx'=8,'sy'=16,'blk'=4] {'sx','sy'}, use_global_device_ids=true, to_apply=%region_0.1 | all-reduce | flops 1024 | bytes 8192 | tf_op jit(solution)/shard_map/psum | solution.py:34
  582.3 0.3 fusion.12
  582.6 0.3 fusion.14
  582.9 0.3 fusion.3
  583.2 0.3 fusion.4
  583.5 0.4 pad_maximum_fusion
  583.9 1.1 copy.50
  585.0 3.5 all-to-all-start.1
  588.4 0.1 copy.40
  588.5 10.6 %all-to-all-done.1 = bf16[4,16,2,2048]{3,1,2,0:T(8,128)(2,1)S(1)} async-done(((bf16[4,16,2,2048]{3,1,2,0:T(8,128)(2,1)}), bf16[4,16,2,2048]{3,1,2,0:T(8,128)(2,1)S(1)}, u32[]{:S(2)}, u32[]{:S(2)}) %all-to-all-start.1) | async-done | bytes 524320 | tf_op jit(solution)/shard_map/all_to_all | solution.py:58
  599.1 0.5 copy.51
  599.7 0.2 reshape.160
  599.9 1.4 fusion
  (8 shorter events, 0.2 us)
Async XLA Ops:
  0.0 1.9 copy-start
  2.4 12.1 %copy-start.3 = (f32[16,8]{0,1:T(8,128)S(1)}, f32[16,8]{0,1:T(8,128)}, u32[]{:S(2)}) copy-start(f32[16,8]{0,1:T(8,128)} %param.11) | copy-start | bytes 1540
  3.5 23.1 %copy-start.2 = (f32[2048]{0:T(1024)S(1)}, f32[2048]{0:T(1024)}, u32[]{:S(2)}) copy-start(f32[2048]{0:T(1024)} %param.10) | copy-start | bytes 24580
  3.5 22.9 %all-to-all-start = ((bf16[1,64,2,2048]{3,2,0,1:T(2,128)(2,1)}), bf16[1,64,2,2048]{3,2,0,1:T(2,128)(2,1)S(1)}, u32[]{:S(2)}, u32[]{:S(2)}) async-start(bf16[1,64,2,2048]{3,2,0,1:T(2,128)(2,1)} %bitcast.2), calls=%async_computation | async-start | bytes 1048576 | tf_op jit(solution)/shard_map/all_to_all | solution.py:56
  14.5 12.2 %copy-start.1 = (bf16[16,2,8,2048]{3,2,1,0:T(8,128)(2,1)S(1)}, bf16[16,2,8,2048]{3,2,1,0:T(8,128)(2,1)}, u32[]{:S(2)}) copy-start(bf16[16,2,8,2048]{3,2,1,0:T(8,128)(2,1)} %param.9) | copy-start | bytes 3145732
  585.0 14.2 %all-to-all-start.1 = ((bf16[4,16,2,2048]{3,1,2,0:T(8,128)(2,1)}), bf16[4,16,2,2048]{3,1,2,0:T(8,128)(2,1)S(1)}, u32[]{:S(2)}, u32[]{:S(2)}) async-start(bf16[4,16,2,2048]{3,1,2,0:T(8,128)(2,1)} %copy.50), calls=%async_computation.1 | async-start | bytes 1048576 | tf_op jit(solution)/shard_map/all_to_all | solution.py:58
where the time goes:
time: 604 us; the launch traced here: 601 us
  blocking collectives  553 us (92%)
  waiting for transfers between devices  22.4 us (4%)
  starting transfers between devices  14.4 us (2%)
    psum x1, blocking collectives, project_filter(): summed = lax.psum(local_sums, ('sx', 'sy'))  553 us
  transfers between devices with their start and end apart: 2, of which 2 were waited for; matrix products, arithmetic and copies ran while one was open for 0% of the time, Pallas kernels for 0%

commit v1 on v0

v1 whole, which is shorter than its diff:
```python
import functools
import math

import jax
import jax.numpy as jnp
from jax import lax
from jax.experimental import pallas as pl
from jax.experimental.pallas import tpu as pltpu
from jax.sharding import PartitionSpec as P

NFFT = 256
NF = 64
K = 8
NB = 4
Q = 2
GROUP = NF // NB
J = GROUP // Q
RB = 2 * J
RQ = NB * RB
MQ = J * 2 * K
TILE = 512
MESH = pl.DeviceIdType.MESH


def unit_cosine(step):
    folded = jnp.minimum(step, 256 - step)
    x = (64 - folded).astype(jnp.float32) * (math.pi / 128)
    y = x * x
    poly = 1.0 / 362880 - y * (1.0 / 39916800)
    poly = -1.0 / 5040 + y * poly
    poly = 1.0 / 120 + y * poly
    poly = -1.0 / 6 + y * poly
    return x + x * y * poly


def row_frequency(row, me):
    partner = (row // RB) % NB
    return ((me + partner) % NB) * GROUP + (row // RQ) * J + row % J


def row_part(row):
    return (row // J) % 2


def kernel(
    sizes, cells_all, off_ref, freqs_ref, gain_ref, cw_ref, snap_hbm, modes_hbm,
    ret_ref, inv_ref,
    snap, modes, tab, spec, recv, reb, own, first, second,
    load_sem, fsend, frecv, rsend, rrecv, psend, precv, out_sem,
):
    nx, ny = sizes
    me, ix, iy = lax.axis_index("blk"), lax.axis_index("sx"), lax.axis_index("sy")
    cells = snap.shape[1]

    load_snap = pltpu.make_async_copy(snap_hbm.at[0], snap, load_sem.at[0])
    load_modes = pltpu.make_async_copy(modes_hbm, modes, load_sem.at[1])
    load_snap.start()
    load_modes.start()

    barrier = pltpu.get_barrier_semaphore()
    for d in range(1, NB):
        pl.semaphore_signal(barrier, inc=1, device_id={"blk": (me + d) % NB}, device_id_type=MESH)

    @pl.loop(1, ny)
    def _(d):
        pl.semaphore_signal(barrier, inc=1, device_id={"sy": lax.rem(iy + d, ny)}, device_id_type=MESH)

    @pl.loop(1, nx)
    def _(d):
        pl.semaphore_signal(barrier, inc=1, device_id={"sx": lax.rem(ix + d, nx)}, device_id_type=MESH)

    rows, seg = tab.shape
    fr = jnp.broadcast_to(freqs_ref[...].astype(jnp.float32), (rows, NF))
    row = lax.broadcasted_iota(jnp.int32, (rows, NF), 0)
    hit = lax.broadcasted_iota(jnp.int32, (rows, NF), 1) == row_frequency(row, me)
    fcol = jnp.sum(jnp.where(hit, fr, 0.0), axis=1, keepdims=True).astype(jnp.int32)
    part = row_part(lax.broadcasted_iota(jnp.int32, (rows, 1), 0))
    time = lax.broadcasted_iota(jnp.int32, (rows, seg), 1) - off_ref[0]
    value = unit_cosine((fcol * time + 64 * part) & 255) * (1.0 / math.sqrt(NFFT))
    inside = (time >= 0) & (time < NFFT)
    tab[...] = jnp.where(inside, value, 0.0).astype(jnp.bfloat16)

    load_snap.wait()

    def forward_copy(q, d):
        return pltpu.make_async_remote_copy(
            src_ref=spec.at[pl.ds(q * RQ + d * RB, RB)],
            dst_ref=recv.at[pl.ds(q * RQ + d * RB, RB)],
            send_sem=fsend.at[q, d], recv_sem=frecv.at[q, d],
            device_id={"blk": (me + d) % NB}, device_id_type=MESH,
        )

    def back_copy(q, d):
        return pltpu.make_async_remote_copy(
            src_ref=reb.at[pl.ds(q * RQ + d * RB, RB)],
            dst_ref=ret_ref.at[pl.ds(q * RQ + d * RB, RB)],
            send_sem=rsend.at[q, d], recv_sem=rrecv.at[q, d],
            device_id={"blk": (me + NB - d) % NB}, device_id_type=MESH,
        )

    for q in range(Q):
        rows_q = pl.ds(q * RQ, RQ)
        for c in range(0, cells, TILE):
            s = jnp.dot(
                tab[rows_q, :], snap[:, pl.ds(c, TILE)], preferred_element_type=jnp.float32
            ).astype(jnp.bfloat16)
            spec[rows_q, pl.ds(c, TILE)] = s
        if q == 0:
            pl.semaphore_wait(barrier, NB - 1 + ny - 1 + nx - 1)
        for d in (2, 1, 3):
            forward_copy(q, d).start()

    sel_row = lax.broadcasted_iota(jnp.int32, (NF, rows), 1)
    sel = lax.broadcasted_iota(jnp.int32, (NF, rows), 0) == row_frequency(sel_row, me)
    fb = jnp.broadcast_to(freqs_ref[...], (8, NF)).astype(jnp.float32).astype(jnp.bfloat16)
    flane = jnp.dot(
        fb, sel.astype(jnp.float32).astype(jnp.bfloat16), preferred_element_type=jnp.float32
    )[0:1].astype(jnp.int32)
    part = row_part(lax.broadcasted_iota(jnp.int32, (1, rows), 1))
    time = lax.broadcasted_iota(jnp.int32, (NFFT, rows), 0)
    inv_ref[...] = (
        unit_cosine((flane * time + 64 * part) & 255) * (1.0 / math.sqrt(NF))
    ).astype(jnp.bfloat16)

    lane = lax.broadcasted_iota(jnp.int32, (K, Q * MQ), 1)
    spread = (lane % K == lax.broadcasted_iota(jnp.int32, (K, Q * MQ), 0)).astype(jnp.float32)
    wide = jnp.dot(
        gain_ref[...], spread, precision=lax.Precision.HIGHEST, preferred_element_type=jnp.float32
    )
    lane = lax.broadcasted_iota(jnp.int32, (GROUP, Q * MQ), 1)
    mine = lane // (2 * K) == lax.broadcasted_iota(jnp.int32, (GROUP, Q * MQ), 0)
    gains = jnp.sum(jnp.where(mine, wide, 0.0), axis=0, keepdims=True)
    lane = lax.broadcasted_iota(jnp.int32, (J, MQ), 1)
    diagonal = lane // (2 * K) == lax.broadcasted_iota(jnp.int32, (J, MQ), 0)
    lane8 = lax.broadcasted_iota(jnp.int32, (2 * NB, MQ), 1)
    side = (lane8 // K) % 2
    turn = lax.broadcasted_iota(jnp.int32, (2 * NB, MQ), 0) % 2
    scale = 1.0 / math.sqrt(cells_all)

    load_modes.wait()

    def exchange(q, stage, axis, n, index, buffer):
        @pl.loop(1, n)
        def _(d):
            pltpu.make_async_remote_copy(
                src_ref=own.at[q, stage], dst_ref=buffer.at[q, d - 1],
                send_sem=psend.at[q, stage], recv_sem=precv.at[q, stage],
                device_id={axis: lax.rem(index + d, n)}, device_id_type=MESH,
            ).start()

        pltpu.make_async_copy(buffer.at[q], buffer.at[q], precv.at[q, stage]).wait()
        return own[q, stage] + jnp.sum(buffer[q], axis=0)

    for q in range(Q):
        rows_q = pl.ds(q * RQ, RQ)
        modes_q = pl.ds(q * MQ, MQ)
        for d in range(1, NB):
            forward_copy(q, d).wait_recv()
        product = jnp.zeros((RQ, MQ), jnp.float32)
        for c in range(0, cells, TILE):
            cols = pl.ds(c, TILE)
            local = spec[pl.ds(q * RQ, RB), cols]
            others = recv[pl.ds(q * RQ + RB, RQ - RB), cols]
            x = jnp.concatenate([local, others], axis=0)
            weighted = (x.astype(jnp.float32) * cw_ref[:, cols]).astype(jnp.bfloat16)
            product += lax.dot_general(
                weighted, modes[modes_q, cols], (((1,), (1,)), ((), ())),
                preferred_element_type=jnp.float32,
            )
        product = product.reshape(2 * NB, J, MQ)
        coeff = jnp.sum(jnp.where(diagonal[None], product, 0.0), axis=1)
        own[q, 0] = coeff
        own[q, 1] = exchange(q, 0, "sy", ny, iy, first)
        total = exchange(q, 1, "sx", nx, ix, second)
        crossed = jnp.where(side == 0, pltpu.roll(total, MQ - K, 1), pltpu.roll(total, K, 1))
        crossed = jnp.where(turn == 0, pltpu.roll(crossed, 2 * NB - 1, 0), pltpu.roll(crossed, 1, 0))
        both = jnp.where(side == turn, total + crossed, total - crossed)
        scaled = gains[:, q * MQ : (q + 1) * MQ] * (both * scale)
        table = jnp.where(diagonal[None], scaled[:, None, :], 0.0).reshape(RQ, MQ)
        table = table.astype(jnp.bfloat16)
        for c in range(0, cells, TILE):
            cols = pl.ds(c, TILE)
            reb[rows_q, cols] = jnp.dot(
                table, modes[modes_q, cols], preferred_element_type=jnp.float32
            ).astype(jnp.bfloat16)
        for d in (2, 1, 3):
            back_copy(q, d).start()
        pltpu.make_async_copy(
            reb.at[pl.ds(q * RQ, RB)], ret_ref.at[pl.ds(q * RQ, RB)], out_sem.at[q]
        ).start()

    for q in range(Q):
        for d in range(1, NB):
            forward_copy(q, d).wait_send()
            back_copy(q, d).wait()
        pltpu.make_async_copy(
            reb.at[pl.ds(q * RQ, RB)], ret_ref.at[pl.ds(q * RQ, RB)], out_sem.at[q]
        ).wait()
        for stage, buffer in ((0, first), (1, second)):
            pltpu.make_async_copy(buffer.at[q], buffer.at[q], psend.at[q, stage]).wait()


def inverse_kernel(inv_ref, ret_ref, out_ref):
    out_ref[0] = jnp.dot(
        inv_ref[...], ret_ref[...], preferred_element_type=jnp.float32
    ).astype(jnp.bfloat16)


def solution(mesh):
    nx, ny = mesh.shape["sx"], mesh.shape["sy"]

    def per_device(snapshots, offsets, freqs, modes, cell_weights, filter_weights):
        seg, cells = snapshots.shape[1:]
        vmem = pl.BlockSpec(memory_space=pltpu.VMEM)
        anywhere = pl.BlockSpec(memory_space=pl.ANY)
        bf16 = jnp.bfloat16
        returned, inverse = pl.pallas_call(
            functools.partial(kernel, (nx, ny), cells * nx * ny),
            out_shape=(
                jax.ShapeDtypeStruct((2 * NF, cells), bf16),
                jax.ShapeDtypeStruct((NFFT, 2 * NF), bf16),
            ),
            in_specs=[
                pl.BlockSpec(memory_space=pltpu.SMEM), vmem, vmem, vmem, anywhere, anywhere,
            ],
            out_specs=(anywhere, vmem),
            scratch_shapes=[
                pltpu.VMEM((seg, cells), bf16),
                pltpu.VMEM((GROUP * 2 * K, cells), bf16),
                pltpu.VMEM((2 * NF, seg), bf16),
                pltpu.VMEM((2 * NF, cells), bf16),
                pltpu.VMEM((2 * NF, cells), bf16),
                pltpu.VMEM((2 * NF, cells), bf16),
                pltpu.VMEM((Q, 2, 2 * NB, MQ), jnp.float32),
                pltpu.VMEM((Q, ny - 1, 2 * NB, MQ), jnp.float32),
                pltpu.VMEM((Q, nx - 1, 2 * NB, MQ), jnp.float32),
                pltpu.SemaphoreType.DMA((2,)),
                pltpu.SemaphoreType.DMA((Q, NB)),
                pltpu.SemaphoreType.DMA((Q, NB)),
                pltpu.SemaphoreType.DMA((Q, NB)),
                pltpu.SemaphoreType.DMA((Q, NB)),
                pltpu.SemaphoreType.DMA((Q, 2)),
                pltpu.SemaphoreType.DMA((Q, 2)),
                pltpu.SemaphoreType.DMA((Q,)),
            ],
            compiler_params=pltpu.CompilerParams(
                collective_id=0, has_side_effects=True, vmem_limit_bytes=48 * 2**20
            ),
            name="exchange",
        )(
            offsets, freqs.reshape(1, NF), filter_weights, cell_weights.reshape(1, cells),
            snapshots, modes.reshape(GROUP * 2 * K, cells),
        )
        tile = min(1024, cells)
        return pl.pallas_call(
            inverse_kernel,
            grid=(cells // tile,),
            out_shape=jax.ShapeDtypeStruct((1, NFFT, cells), bf16),
            in_specs=[
                pl.BlockSpec((NFFT, 2 * NF), lambda i: (0, 0)),
                pl.BlockSpec((2 * NF, tile), lambda i: (0, i)),
            ],
            out_specs=pl.BlockSpec((1, NFFT, tile), lambda i: (0, 0, i)),
            name="inverse",
        )(inverse, returned)

    placed = (
        P("blk", None, ("sx", "sy")),
        P("blk"),
        P(),
        P("blk", None, None, ("sx", "sy")),
        P(("sx", "sy")),
        P("blk", None),
    )
    return jax.shard_map(
        per_device, mesh=mesh, in_specs=placed,
        out_specs=P("blk", None, ("sx", "sy")), check_vma=False,
    )
```

time: 604 us -> 64.4 us (0.11)
  the two profiles are of different devices: /device:TPU:1 before, /device:TPU:2 now
where the time goes in v1:
time: 64.4 us; the launch traced here: 64.1 us
  Pallas kernels  57.3 us (89%)
  local copies, waits for them, and re-layouts  6.06 us (9%)
  between operations  0.67 us (1%)
    pallas_call x1, Pallas kernels, per_device(): pl.pallas_call(functools.partial(kernel, (nx, ny), cells * nx * ny), out_...  55 us
    unnamed x13, local copies, waits for them, and re-layouts  6.06 us
    pallas_call x1, Pallas kernels, per_device(): pl.pallas_call(inverse_kernel, grid=(cells // tile,), out_shape=jax.Shape...  2.32 us

profile of v1, /device:TPU:2, one launch (start us, length us, event | category | flops | bytes accessed | tf_op | source)
XLA Modules:
  0.0 64.1 jit_solution(15385093334550398746)
XLA Ops:
  0.7 0.8 %copy.7.gain_ref = f32[16,8]{1,0:T(8,128)S(1)} copy(f32[16,8]{0,1:T(8,128)} %param.11) | data formatting | bytes 1024 | tf_op args[5]
  1.4 0.0 copy-start
  1.4 1.3 %copy-done = bf16[1,320,2048]{2,1,0:T(8,128)(2,1)S(1)} copy-done((bf16[1,320,2048]{2,1,0:T(8,128)(2,1)S(1)}, bf16[1,320,2048]{2,1,0:T(8,128)(2,1)}, u32[]{:S(2)}) %copy-start) | copy-done | bytes 1310744
  2.7 0.0 copy-start.1
  2.7 1.2 %copy-done.1 = bf16[16,2,8,2048]{3,2,1,0:T(8,128)(2,1)S(1)} copy-done((bf16[16,2,8,2048]{3,2,1,0:T(8,128)(2,1)S(1)}, bf16[16,2,8,2048]{3,2,1,0:T(8,128)(2,1)}, u32[]{:S(2)}) %copy-start.1) | copy-done | bytes 1048600
  4.0 0.0 copy-start.4
  4.0 0.7 %copy-done.4 = f32[2048]{0:T(1024)S(1)} copy-done((f32[2048]{0:T(1024)S(1)}, f32[2048]{0:T(1024)}, u32[]{:S(2)}) %copy-start.4) | copy-done | bytes 8216
  4.7 0.0 copy-start.5
  4.7 0.7 %copy-done.5 = s32[64]{0:T(128)S(1)} copy-done((s32[64]{0:T(128)S(1)}, s32[64]{0:T(128)}, u32[]{:S(2)}) %copy-start.5) | copy-done | bytes 280
  5.3 55.0 %exchange.1 = (bf16[128,2048]{1,0:T(8,128)(2,1)S(1)}, bf16[256,128]{1,0:T(8,128)(2,1)S(1)}) custom-call(s32[1]{0:T(128)S(6)} %copy.8.off_ref, s32[1,64]{1,0:T(1,128)S(1)} %bitcast.5, f32[16,8]{1,0:T(8,128)S(1)} %copy.7.gain_ref, f32[1,2048]{1,0:T(1,128)S(1)} %bitcast.4, bf16[1,320,2048]{2,1,0:T(8,128)(2,1)S(1)} %copy-done, bf16[256,2048]{1,0:T(8,128)(2,1)S(1)} %bitcast.3), custom_call_target="tpu_custom_call" | custom-call | tf_op jit(solution)/shard_map/exchange/pallas_call | solution.py:217
  60.3 0.0 copy-start.2
  60.4 0.8 %copy-done.2 = bf16[128,2048]{1,0:T(8,128)(2,1)} copy-done((bf16[128,2048]{1,0:T(8,128)(2,1)}, bf16[128,2048]{1,0:T(8,128)(2,1)S(1)}, u32[]{:S(2)}) %copy-start.2) | copy-done | bytes 524312
  61.1 0.0 copy-start.3
  61.1 0.6 copy-done.3
  61.8 2.3 %inverse.1 = bf16[1,256,2048]{2,1,0:T(8,128)(2,1)} custom-call(bf16[256,128]{1,0:T(8,128)(2,1)} %copy-done.3, bf16[128,2048]{1,0:T(8,128)(2,1)} %copy-done.2), custom_call_target="tpu_custom_call" | custom-call | tf_op jit(solution)/shard_map/inverse/pallas_call | solution.py:255
Async XLA Ops:
  1.4 1.3 %copy-start = (bf16[1,320,2048]{2,1,0:T(8,128)(2,1)S(1)}, bf16[1,320,2048]{2,1,0:T(8,128)(2,1)}, u32[]{:S(2)}) copy-start(bf16[1,320,2048]{2,1,0:T(8,128)(2,1)} %snap_hbm.1) | copy-start | bytes 3932164
  2.7 1.2 %copy-start.1 = (bf16[16,2,8,2048]{3,2,1,0:T(8,128)(2,1)S(1)}, bf16[16,2,8,2048]{3,2,1,0:T(8,128)(2,1)}, u32[]{:S(2)}) copy-start(bf16[16,2,8,2048]{3,2,1,0:T(8,128)(2,1)} %param.9) | copy-start | bytes 3145732
  4.0 0.7 %copy-start.4 = (f32[2048]{0:T(1024)S(1)}, f32[2048]{0:T(1024)}, u32[]{:S(2)}) copy-start(f32[2048]{0:T(1024)} %param.10) | copy-start | bytes 24580
  4.7 0.7 %copy-start.5 = (s32[64]{0:T(128)S(1)}, s32[64]{0:T(128)}, u32[]{:S(2)}) copy-start(s32[64]{0:T(128)} %param.8) | copy-start | bytes 772
  60.3 0.8 %copy-start.2 = (bf16[128,2048]{1,0:T(8,128)(2,1)}, bf16[128,2048]{1,0:T(8,128)(2,1)S(1)}, u32[]{:S(2)}) copy-start(bf16[128,2048]{1,0:T(8,128)(2,1)S(1)} %get-tuple-element.8.ret_ref) | copy-start | bytes 1572868
  61.1 0.6 copy-start.3

commit v2 on v1

v2 whole, which is shorter than its diff:
```python
import functools
import math

import jax
import jax.numpy as jnp
from jax import lax
from jax.experimental import pallas as pl
from jax.experimental.pallas import tpu as pltpu
from jax.sharding import PartitionSpec as P

NFFT = 256
NF = 64
K = 8
NB = 4
Q = 4
GROUP = NF // NB
J = GROUP // Q
E = 2 * J
H = 2
RB = H * E
RQ = NB * RB
TQ = NB * E
LANES = 128
TILE = 512
MESH = pl.DeviceIdType.MESH


def unit_cosine(step):
    folded = jnp.minimum(step, 256 - step)
    x = (64 - folded).astype(jnp.float32) * (math.pi / 128)
    y = x * x
    poly = 1.0 / 362880 - y * (1.0 / 39916800)
    poly = -1.0 / 5040 + y * poly
    poly = 1.0 / 120 + y * poly
    poly = -1.0 / 6 + y * poly
    return x + x * y * poly


def row_frequency(row, me):
    partner = (row // E) % NB
    return ((me + partner) % NB) * GROUP + (row // TQ) * J + row % J


def row_part(row):
    return (row // J) % 2


def halves_together(parts):
    return jnp.concatenate(
        [parts[h][d * E : (d + 1) * E] for d in range(NB) for h in range(H)], axis=0
    )


def sum_of_four(x, j):
    x = x + jnp.where(j == J - 1, pltpu.roll(x, J - 1, 0), pltpu.roll(x, E - 1, 0))
    return x + jnp.where(j >= 2, pltpu.roll(x, 2, 0), pltpu.roll(x, E - 2, 0))


def kernel(
    sizes, cells_all, off_ref, freqs_hbm, gain_hbm, cw_hbm, snap_hbm, modes_hbm,
    ret_ref, inv_ref,
    freqs_ref, gain_ref, cw_ref, snap, modes,
    tab, spec, recv, reb, own, first, second,
    load_sem, fsend, frecv, rsend, rrecv, psend, precv, out_sem,
):
    nx, ny = sizes
    me, ix, iy = lax.axis_index("blk"), lax.axis_index("sx"), lax.axis_index("sy")
    half = spec.shape[1]

    loads = [
        pltpu.make_async_copy(src, dst, load_sem.at[i])
        for i, (src, dst) in enumerate(
            (
                (freqs_hbm, freqs_ref), (snap_hbm.at[0], snap),
                (gain_hbm, gain_ref), (cw_hbm, cw_ref), (modes_hbm, modes),
            )
        )
    ]
    for load in loads:
        load.start()

    barrier = pltpu.get_barrier_semaphore()
    for d in range(1, NB):
        pl.semaphore_signal(barrier, inc=1, device_id={"blk": (me + d) % NB}, device_id_type=MESH)

    @pl.loop(1, nx)
    def _(d):
        pl.semaphore_signal(barrier, inc=1, device_id={"sx": lax.rem(ix + d, nx)}, device_id_type=MESH)

    @pl.loop(1, ny)
    def _(d):
        pl.semaphore_signal(barrier, inc=1, device_id={"sy": lax.rem(iy + d, ny)}, device_id_type=MESH)

    loads[0].wait()
    rows, seg = tab.shape
    fr = jnp.broadcast_to(freqs_ref[...].astype(jnp.float32), (rows, NF))
    row = lax.broadcasted_iota(jnp.int32, (rows, NF), 0)
    hit = lax.broadcasted_iota(jnp.int32, (rows, NF), 1) == row_frequency(row, me)
    fcol = jnp.sum(jnp.where(hit, fr, 0.0), axis=1, keepdims=True).astype(jnp.int32)
    part = row_part(lax.broadcasted_iota(jnp.int32, (rows, 1), 0))
    time = lax.broadcasted_iota(jnp.int32, (rows, seg), 1) - off_ref[0]
    value = unit_cosine((fcol * time + 64 * part) & 255) * (1.0 / math.sqrt(NFFT))
    inside = (time >= 0) & (time < NFFT)
    tab[...] = jnp.where(inside, value, 0.0).astype(jnp.bfloat16)

    def forward_copy(q, d):
        return pltpu.make_async_remote_copy(
            src_ref=spec.at[pl.ds(q * RQ + d * RB, RB)],
            dst_ref=recv.at[pl.ds(q * RQ + d * RB, RB)],
            send_sem=fsend.at[q, d], recv_sem=frecv.at[q, d],
            device_id={"blk": (me + d) % NB}, device_id_type=MESH,
        )

    def back_copy(q, d):
        return pltpu.make_async_remote_copy(
            src_ref=reb.at[pl.ds(q * RQ + d * RB, RB)],
            dst_ref=ret_ref.at[pl.ds(q * RQ + d * RB, RB)],
            send_sem=rsend.at[q, d], recv_sem=rrecv.at[q, d],
            device_id={"blk": (me + NB - d) % NB}, device_id_type=MESH,
        )

    def transform(q):
        for c in range(0, half, TILE):
            parts = [
                jnp.dot(
                    tab[pl.ds(q * TQ, TQ), :], snap[:, pl.ds(h * half + c, TILE)],
                    preferred_element_type=jnp.float32,
                )
                for h in range(H)
            ]
            spec[pl.ds(q * RQ, RQ), pl.ds(c, TILE)] = halves_together(parts).astype(jnp.bfloat16)

    def send_forward(q):
        for d in (2, 1, 3):
            if q:
                forward_copy(q - 1, d).wait_send()
            forward_copy(q, d).start()

    loads[1].wait()
    transform(0)
    pl.semaphore_wait(barrier, NB - 1 + ny - 1 + nx - 1)
    send_forward(0)
    for q in range(1, Q):
        transform(q)

    sel_row = lax.broadcasted_iota(jnp.int32, (NF, rows), 1)
    sel = lax.broadcasted_iota(jnp.int32, (NF, rows), 0) == row_frequency(sel_row, me)
    fb = jnp.broadcast_to(freqs_ref[...], (8, NF)).astype(jnp.float32).astype(jnp.bfloat16)
    flane = jnp.dot(
        fb, sel.astype(jnp.float32).astype(jnp.bfloat16), preferred_element_type=jnp.float32
    )[0:1].astype(jnp.int32)
    part = row_part(lax.broadcasted_iota(jnp.int32, (1, rows), 1))
    time = lax.broadcasted_iota(jnp.int32, (NFFT, rows), 0)
    inv_ref[...] = (
        unit_cosine((flane * time + 64 * part) & 255) * (1.0 / math.sqrt(NF))
    ).astype(jnp.bfloat16)

    send_forward(1)

    loads[2].wait()
    all_lanes = GROUP * 2 * K
    lane = lax.broadcasted_iota(jnp.int32, (K, all_lanes), 1)
    spread = (lane % K == lax.broadcasted_iota(jnp.int32, (K, all_lanes), 0)).astype(jnp.float32)
    wide = lax.dot_general(
        gain_ref[...], spread, (((0,), (0,)), ((), ())),
        precision=lax.Precision.HIGHEST, preferred_element_type=jnp.float32,
    )
    lane = lax.broadcasted_iota(jnp.int32, (GROUP, all_lanes), 1)
    mine = lane // (2 * K) == lax.broadcasted_iota(jnp.int32, (GROUP, all_lanes), 0)
    gains = jnp.sum(jnp.where(mine, wide, 0.0), axis=0, keepdims=True)

    row = lax.broadcasted_iota(jnp.int32, (E, LANES), 0)
    lane = lax.broadcasted_iota(jnp.int32, (E, LANES), 1)
    j, turn, side = row % J, row // J, (lane // K) % 2
    scale = 1.0 / math.sqrt(cells_all)

    def diagonal(q):
        return lane // (2 * K) == (q % 2) * J + j

    loads[3].wait()
    loads[4].wait()

    def spread_out(q, stage, axis, n, index, buffer):
        @pl.loop(1, n)
        def _(d):
            pltpu.make_async_remote_copy(
                src_ref=own.at[q, stage], dst_ref=buffer.at[q, d - 1],
                send_sem=psend.at[q, stage], recv_sem=precv.at[q, stage],
                device_id={axis: lax.rem(index + d, n)}, device_id_type=MESH,
            ).start()

    def total_of(q, stage, buffer):
        pltpu.make_async_copy(buffer.at[q], buffer.at[q], precv.at[q, stage]).wait()
        return own[q, stage] + jnp.sum(buffer[q], axis=0)

    def project(q):
        for d in range(1, NB):
            forward_copy(q, d).wait_recv()
        modes_q = pl.ds(q // 2 * LANES, LANES)
        product = jnp.zeros((TQ, LANES), jnp.float32)
        for c in range(0, half, TILE):
            cols = pl.ds(c, TILE)
            x = jnp.concatenate(
                [spec[pl.ds(q * RQ, RB), cols], recv[pl.ds(q * RQ + RB, RQ - RB), cols]], axis=0
            ).astype(jnp.float32)
            for h in range(H):
                cells = pl.ds(h * half + c, TILE)
                xh = jnp.concatenate(
                    [x[(d * H + h) * E : (d * H + h + 1) * E] for d in range(NB)], axis=0
                )
                product += lax.dot_general(
                    (xh * cw_ref[:, cells]).astype(jnp.bfloat16), modes[modes_q, cells],
                    (((1,), (1,)), ((), ())), preferred_element_type=jnp.float32,
                )
        coeff = jnp.zeros((E, LANES), jnp.float32)
        for d in range(NB):
            sums = sum_of_four(jnp.where(diagonal(q), product[d * E : (d + 1) * E], 0.0), j)
            coeff += jnp.where(j == d, sums, 0.0)
        own[q, 0] = coeff
        spread_out(q, 0, "sy", ny, iy, first)

    def pass_on(q):
        own[q, 1] = total_of(q, 0, first)
        spread_out(q, 1, "sx", nx, ix, second)

    def rebuild(q):
        total = total_of(q, 1, second)
        crossed = jnp.where(
            side == 0, pltpu.roll(total, LANES - K, 1), pltpu.roll(total, K, 1)
        )
        crossed = pltpu.roll(crossed, J, 0)
        both = jnp.where(side == turn, total + crossed, total - crossed)
        scaled = gains[:, q // 2 * LANES : (q // 2 + 1) * LANES] * (both * scale)
        table = jnp.concatenate(
            [
                jnp.where(diagonal(q), sum_of_four(jnp.where(j == d, scaled, 0.0), j), 0.0)
                for d in range(NB)
            ],
            axis=0,
        ).astype(jnp.bfloat16)
        modes_q = pl.ds(q // 2 * LANES, LANES)
        for c in range(0, half, TILE):
            parts = [
                jnp.dot(
                    table, modes[modes_q, pl.ds(h * half + c, TILE)],
                    preferred_element_type=jnp.float32,
                )
                for h in range(H)
            ]
            reb[pl.ds(q * RQ, RQ), pl.ds(c, TILE)] = halves_together(parts).astype(jnp.bfloat16)
        for d in (2, 1, 3):
            back_copy(q, d).start()
        keep(q).start()

    def keep(q):
        return pltpu.make_async_copy(
            reb.at[pl.ds(q * RQ, RB)], ret_ref.at[pl.ds(q * RQ, RB)], out_sem.at[q]
        )

    send_forward(2)
    send_forward(3)
    project(0)
    project(1)
    pass_on(0)
    project(2)
    pass_on(1)
    project(3)
    rebuild(0)
    pass_on(2)
    rebuild(1)
    pass_on(3)
    rebuild(2)
    rebuild(3)

    for d in range(1, NB):
        forward_copy(Q - 1, d).wait_send()
    for q in range(Q):
        for stage, buffer in ((0, first), (1, second)):
            pltpu.make_async_copy(buffer.at[q], buffer.at[q], psend.at[q, stage]).wait()
        for d in range(1, NB):
            back_copy(q, d).wait()
        keep(q).wait()


def inverse_kernel(inv_ref, ret_ref, out_ref):
    tile = out_ref.shape[2]
    per_half = ret_ref.shape[1] // tile
    step = pl.program_id(0)
    cols = pl.ds(pl.multiple_of(lax.rem(step, per_half) * tile, tile), tile)
    x = ret_ref[:, cols].astype(jnp.float32).reshape(Q * NB, H, E, tile)
    x = jnp.where(step < per_half, x[:, 0], x[:, 1]).reshape(2 * NF, tile)
    out_ref[0] = jnp.dot(
        inv_ref[...], x.astype(jnp.bfloat16), preferred_element_type=jnp.float32
    ).astype(jnp.bfloat16)


def solution(mesh):
    nx, ny = mesh.shape["sx"], mesh.shape["sy"]

    def per_device(snapshots, offsets, freqs, modes, cell_weights, filter_weights):
        seg, cells = snapshots.shape[1:]
        half = cells // H
        vmem = pl.BlockSpec(memory_space=pltpu.VMEM)
        hbm = pl.BlockSpec(memory_space=pltpu.HBM)
        bf16, f32, dma = jnp.bfloat16, jnp.float32, pltpu.SemaphoreType.DMA
        returned, inverse = pl.pallas_call(
            functools.partial(kernel, (nx, ny), cells * nx * ny),
            out_shape=(
                jax.ShapeDtypeStruct((Q * RQ, half), bf16),
                jax.ShapeDtypeStruct((NFFT, 2 * NF), bf16),
            ),
            in_specs=[pl.BlockSpec(memory_space=pltpu.SMEM)] + [hbm] * 5,
            out_specs=(vmem, vmem),
            scratch_shapes=[
                pltpu.VMEM((1, NF), jnp.int32),
                pltpu.VMEM((K, GROUP), f32),
                pltpu.VMEM((1, cells), f32),
                pltpu.VMEM((seg, cells), bf16),
                pltpu.VMEM((GROUP * 2 * K, cells), bf16),
                pltpu.VMEM((2 * NF, seg), bf16),
                pltpu.VMEM((Q * RQ, half), bf16),
                pltpu.VMEM((Q * RQ, half), bf16),
                pltpu.VMEM((Q * RQ, half), bf16),
                pltpu.VMEM((Q, 2, E, LANES), f32),
                pltpu.VMEM((Q, ny - 1, E, LANES), f32),
                pltpu.VMEM((Q, nx - 1, E, LANES), f32),
                dma((5,)), dma((Q, NB)), dma((Q, NB)), dma((Q, NB)), dma((Q, NB)),
                dma((Q, 2)), dma((Q, 2)), dma((Q,)),
            ],
            compiler_params=pltpu.CompilerParams(
                collective_id=0, has_side_effects=True, vmem_limit_bytes=32 * 2**20
            ),
            name="exchange",
        )(
            offsets,
            *(
                pltpu.with_memory_space_constraint(x, pltpu.HBM)
                for x in (
                    freqs.reshape(1, NF), filter_weights.T, cell_weights.reshape(1, cells),
                    snapshots, modes.reshape(GROUP * 2 * K, cells),
                )
            ),
        )
        tile = min(TILE, half)
        return pl.pallas_call(
            inverse_kernel,
            grid=(cells // tile,),
            out_shape=jax.ShapeDtypeStruct((1, NFFT, cells), bf16),
            in_specs=[vmem, vmem],
            out_specs=pl.BlockSpec((1, NFFT, tile), lambda i: (0, 0, i)),
            compiler_params=pltpu.CompilerParams(vmem_limit_bytes=16 * 2**20),
            name="inverse",
        )(inverse, returned)

    placed = (
        P("blk", None, ("sx", "sy")),
        P("blk"),
        P(),
        P("blk", None, None, ("sx", "sy")),
        P(("sx", "sy")),
        P("blk", None),
    )
    return jax.shard_map(
        per_device, mesh=mesh, in_specs=placed,
        out_specs=P("blk", None, ("sx", "sy")), check_vma=False,
    )
```

time: 64.4 us -> 51.1 us (0.79)
  the two profiles are of different devices: /device:TPU:2 before, /device:TPU:1 now
where the time goes in v2:
time: 51.1 us; the launch traced here: 50.9 us
  Pallas kernels  50.2 us (98%)
  between operations  0.66 us (1%)
    pallas_call x1, Pallas kernels, per_device(): pl.pallas_call(functools.partial(kernel, (nx, ny), cells * nx * ny), out_...  48.1 us
    pallas_call x1, Pallas kernels, per_device(): pl.pallas_call(inverse_kernel, grid=(cells // tile,), out_shape=jax.Shape...  2.14 us

profile of v2, /device:TPU:1, one launch (start us, length us, event | category | flops | bytes accessed | tf_op | source)
XLA Modules:
  0.0 50.9 jit_solution(63957565605739753)
XLA Ops:
  0.7 48.1 %exchange.1 = (bf16[256,1024]{1,0:T(8,128)(2,1)S(1)}, bf16[256,128]{1,0:T(8,128)(2,1)S(1)}) custom-call(s32[1]{0:T(128)S(6)} %copy.7.off_ref, s32[1,64]{1,0:T(1,128)} %bitcast.7, f32[8,16]{1,0:T(8,128)} %bitcast.6, f32[1,2048]{1,0:T(1,128)} %bitcast.5, bf16[1,320,2048]{2,1,0:T(8,128)(2,1)} %snap_hbm.1, bf16[256,2048]{1,0:T(8,128)(2,1)} %bitcast.4), custom_call_target="tpu_custom_call" | custom-call | tf_op jit(solution)/shard_map/exchange/pallas_call | solution.py:306
  48.8 2.1 %inverse.1 = bf16[1,256,2048]{2,1,0:T(8,128)(2,1)} custom-call(bf16[256,128]{1,0:T(8,128)(2,1)S(1)} %get-tuple-element.7.inv_ref, bf16[256,1024]{1,0:T(8,128)(2,1)S(1)} %get-tuple-element.8.ret_ref), custom_call_target="tpu_custom_call" | custom-call | tf_op jit(solution)/shard_map/inverse/pallas_call | solution.py:345

commit v3 on v2

--- a/solution.py
+++ b/solution.py
@@ -22,6 +22,7 @@
 TQ = NB * E
 LANES = 128
 TILE = 512
+INNER = 4
 MESH = pl.DeviceIdType.MESH
 
 
@@ -83,25 +84,30 @@
     for d in range(1, NB):
         pl.semaphore_signal(barrier, inc=1, device_id={"blk": (me + d) % NB}, device_id_type=MESH)
 
-    @pl.loop(1, nx)
-    def _(d):
-        pl.semaphore_signal(barrier, inc=1, device_id={"sx": lax.rem(ix + d, nx)}, device_id_type=MESH)
-
-    @pl.loop(1, ny)
-    def _(d):
-        pl.semaphore_signal(barrier, inc=1, device_id={"sy": lax.rem(iy + d, ny)}, device_id_type=MESH)
+    stages = (
+        (first, ny, lambda d: {"sy": (iy + d) % ny}),
+        (second, nx, lambda d: {"sx": (ix + d) % nx}),
+    )
+    greeted = NB - 1
+    for _, n, partner in stages:
+        greeted += n - 1
+        for d in range(1, n):
+            pl.semaphore_signal(barrier, inc=1, device_id=partner(d), device_id_type=MESH)
 
     loads[0].wait()
-    rows, seg = tab.shape
-    fr = jnp.broadcast_to(freqs_ref[...].astype(jnp.float32), (rows, NF))
-    row = lax.broadcasted_iota(jnp.int32, (rows, NF), 0)
-    hit = lax.broadcasted_iota(jnp.int32, (rows, NF), 1) == row_frequency(row, me)
-    fcol = jnp.sum(jnp.where(hit, fr, 0.0), axis=1, keepdims=True).astype(jnp.int32)
-    part = row_part(lax.broadcasted_iota(jnp.int32, (rows, 1), 0))
-    time = lax.broadcasted_iota(jnp.int32, (rows, seg), 1) - off_ref[0]
-    value = unit_cosine((fcol * time + 64 * part) & 255) * (1.0 / math.sqrt(NFFT))
-    inside = (time >= 0) & (time < NFFT)
-    tab[...] = jnp.where(inside, value, 0.0).astype(jnp.bfloat16)
+    rows = tab.shape[0]
+
+    def make_table(start, count):
+        fr = jnp.broadcast_to(freqs_ref[...].astype(jnp.float32), (count, NF))
+        row = lax.broadcasted_iota(jnp.int32, (count, NF), 0) + start
+        hit = lax.broadcasted_iota(jnp.int32, (count, NF), 1) == row_frequency(row, me)
+        fcol = jnp.sum(jnp.where(hit, fr, 0.0), axis=1, keepdims=True).astype(jnp.int32)
+        part = row_part(lax.broadcasted_iota(jnp.int32, (count, 1), 0) + start)
+        time = lax.broadcasted_iota(jnp.int32, (count, NFFT), 1) - off_ref[0]
+        value = unit_cosine((fcol * time + 64 * part) & 255) * (1.0 / math.sqrt(NFFT))
+        tab[pl.ds(start, count)] = value.astype(jnp.bfloat16)
+
+    make_table(0, TQ)
 
     def forward_copy(q, d):
         return pltpu.make_async_remote_copy(
@@ -123,7 +129,7 @@
         for c in range(0, half, TILE):
             parts = [
                 jnp.dot(
-                    tab[pl.ds(q * TQ, TQ), :], snap[:, pl.ds(h * half + c, TILE)],
+                    tab[pl.ds(q * TQ, TQ), :], snap[pl.ds(0, NFFT), pl.ds(h * half + c, TILE)],
                     preferred_element_type=jnp.float32,
                 )
                 for h in range(H)
@@ -137,9 +143,16 @@
             forward_copy(q, d).start()
 
     loads[1].wait()
+    extra = snap.shape[0] - NFFT
+    early = lax.broadcasted_iota(jnp.int32, (extra, TILE), 0) < off_ref[0]
+    for c in range(0, snap.shape[1], TILE):
+        cols = pl.ds(c, TILE)
+        low, high = snap[pl.ds(0, extra), cols], snap[pl.ds(NFFT, extra), cols]
+        snap[pl.ds(0, extra), cols] = jnp.where(early, high, low)
     transform(0)
-    pl.semaphore_wait(barrier, NB - 1 + ny - 1 + nx - 1)
+    pl.semaphore_wait(barrier, greeted)
     send_forward(0)
+    make_table(TQ, rows - TQ)
     for q in range(1, Q):
         transform(q)
 
@@ -180,18 +193,22 @@
     loads[3].wait()
     loads[4].wait()
 
-    def spread_out(q, stage, axis, n, index, buffer):
-        @pl.loop(1, n)
-        def _(d):
+    def spread_out(q, stage):
+        buffer, n, partner = stages[stage]
+        for d in sorted(range(1, n), key=lambda d: abs(d - n // 2)):
             pltpu.make_async_remote_copy(
                 src_ref=own.at[q, stage], dst_ref=buffer.at[q, d - 1],
                 send_sem=psend.at[q, stage], recv_sem=precv.at[q, stage],
-                device_id={axis: lax.rem(index + d, n)}, device_id_type=MESH,
+                device_id=partner(d), device_id_type=MESH,
             ).start()
 
-    def total_of(q, stage, buffer):
-        pltpu.make_async_copy(buffer.at[q], buffer.at[q], precv.at[q, stage]).wait()
-        return own[q, stage] + jnp.sum(buffer[q], axis=0)
+    def total_of(q, stage):
+        buffer, n, _ = stages[stage]
+        total = own[q, stage]
+        if n > 1:
+            pltpu.make_async_copy(buffer.at[q], buffer.at[q], precv.at[q, stage]).wait()
+            total += jnp.sum(buffer[q], axis=0)
+        return total
 
     def project(q):
         for d in range(1, NB):
@@ -217,14 +234,14 @@
             sums = sum_of_four(jnp.where(diagonal(q), product[d * E : (d + 1) * E], 0.0), j)
             coeff += jnp.where(j == d, sums, 0.0)
         own[q, 0] = coeff
-        spread_out(q, 0, "sy", ny, iy, first)
-
-    def pass_on(q):
-        own[q, 1] = total_of(q, 0, first)
-        spread_out(q, 1, "sx", nx, ix, second)
+        spread_out(q, 0)
+
+    def pass_on(q, stage):
+        own[q, stage] = total_of(q, stage - 1)
+        spread_out(q, stage)
 
     def rebuild(q):
-        total = total_of(q, 1, second)
+        total = total_of(q, 1)
         crossed = jnp.where(
             side == 0, pltpu.roll(total, LANES - K, 1), pltpu.roll(total, K, 1)
         )
@@ -248,8 +265,12 @@
                 for h in range(H)
             ]
             reb[pl.ds(q * RQ, RQ), pl.ds(c, TILE)] = halves_together(parts).astype(jnp.bfloat16)
-        for d in (2, 1, 3):
-            back_copy(q, d).start()
+        for b in range(NB):
+
+            @pl.when(b != me)
+            def _():
+                back_copy(q, (me + NB - b) % NB).start()
+
         keep(q).start()
 
     def keep(q):
@@ -257,41 +278,50 @@
             reb.at[pl.ds(q * RQ, RB)], ret_ref.at[pl.ds(q * RQ, RB)], out_sem.at[q]
         )
 
+    project(0)
     send_forward(2)
+    project(1)
     send_forward(3)
-    project(0)
-    project(1)
-    pass_on(0)
+    pass_on(0, 1)
     project(2)
-    pass_on(1)
+    pass_on(1, 1)
     project(3)
     rebuild(0)
-    pass_on(2)
+    pass_on(2, 1)
     rebuild(1)
-    pass_on(3)
+    pass_on(3, 1)
     rebuild(2)
     rebuild(3)
 
     for d in range(1, NB):
         forward_copy(Q - 1, d).wait_send()
     for q in range(Q):
-        for stage, buffer in ((0, first), (1, second)):
-            pltpu.make_async_copy(buffer.at[q], buffer.at[q], psend.at[q, stage]).wait()
+        for stage, (buffer, n, _) in enumerate(stages):
+            if n > 1:
+                pltpu.make_async_copy(buffer.at[q], buffer.at[q], psend.at[q, stage]).wait()
         for d in range(1, NB):
             back_copy(q, d).wait()
         keep(q).wait()
 
 
-def inverse_kernel(inv_ref, ret_ref, out_ref):
-    tile = out_ref.shape[2]
-    per_half = ret_ref.shape[1] // tile
-    step = pl.program_id(0)
-    cols = pl.ds(pl.multiple_of(lax.rem(step, per_half) * tile, tile), tile)
-    x = ret_ref[:, cols].astype(jnp.float32).reshape(Q * NB, H, E, tile)
-    x = jnp.where(step < per_half, x[:, 0], x[:, 1]).reshape(2 * NF, tile)
-    out_ref[0] = jnp.dot(
-        inv_ref[...], x.astype(jnp.bfloat16), preferred_element_type=jnp.float32
-    ).astype(jnp.bfloat16)
+def inverse_kernel(inv_ref, ret_ref, out_hbm, out, sems):
+    half = ret_ref.shape[1]
+    copies = []
+    for c in range(0, half, TILE):
+        x = ret_ref[:, pl.ds(c, TILE)].astype(jnp.float32).reshape(Q * NB, H, E, TILE)
+        for h in range(H):
+            cols = pl.ds(h * half + c, TILE)
+            xh = x[:, h].reshape(2 * NF, TILE).astype(jnp.bfloat16)
+            out[:, cols] = jnp.dot(
+                inv_ref[...], xh, preferred_element_type=jnp.float32
+            ).astype(jnp.bfloat16)
+            copy = pltpu.make_async_copy(
+                out.at[:, cols], out_hbm.at[0, :, cols], sems.at[len(copies)]
+            )
+            copy.start()
+            copies.append(copy)
+    for copy in copies:
+        copy.wait()
 
 
 def solution(mesh):
@@ -317,15 +347,15 @@
                 pltpu.VMEM((1, cells), f32),
                 pltpu.VMEM((seg, cells), bf16),
                 pltpu.VMEM((GROUP * 2 * K, cells), bf16),
-                pltpu.VMEM((2 * NF, seg), bf16),
+                pltpu.VMEM((2 * NF, NFFT), bf16),
                 pltpu.VMEM((Q * RQ, half), bf16),
                 pltpu.VMEM((Q * RQ, half), bf16),
                 pltpu.VMEM((Q * RQ, half), bf16),
-                pltpu.VMEM((Q, 2, E, LANES), f32),
-                pltpu.VMEM((Q, ny - 1, E, LANES), f32),
-                pltpu.VMEM((Q, nx - 1, E, LANES), f32),
+                pltpu.VMEM((Q, 3, E, LANES), f32),
+                pltpu.VMEM((Q, max(ny - 1, 1), E, LANES), f32),
+                pltpu.VMEM((Q, max(nx - 1, 1), E, LANES), f32),
                 dma((5,)), dma((Q, NB)), dma((Q, NB)), dma((Q, NB)), dma((Q, NB)),
-                dma((Q, 2)), dma((Q, 2)), dma((Q,)),
+                dma((Q, 3)), dma((Q, 3)), dma((Q,)),
             ],
             compiler_params=pltpu.CompilerParams(
                 collective_id=0, has_side_effects=True, vmem_limit_bytes=32 * 2**20
@@ -341,13 +371,12 @@
                 )
             ),
         )
-        tile = min(TILE, half)
         return pl.pallas_call(
             inverse_kernel,
-            grid=(cells // tile,),
             out_shape=jax.ShapeDtypeStruct((1, NFFT, cells), bf16),
             in_specs=[vmem, vmem],
-            out_specs=pl.BlockSpec((1, NFFT, tile), lambda i: (0, 0, i)),
+            out_specs=pl.BlockSpec(memory_space=pl.ANY),
+            scratch_shapes=[pltpu.VMEM((NFFT, cells), bf16), dma((cells // TILE,))],
             compiler_params=pltpu.CompilerParams(vmem_limit_bytes=16 * 2**20),
             name="inverse",
         )(inverse, returned)

time: 51.1 us -> 48.2 us (0.943)
  Pallas kernels: 50.2 us -> 47.4 us
    pallas_call x1, Pallas kernels: 48.1 us -> 46.2 us  [per_device(): pl.pallas_call(functools.partial(kernel, (nx, ny), cells * nx * ny), out_...]
    pallas_call x1, Pallas kernels: 2.14 us -> 1.21 us  [per_device(): pl.pallas_call(inverse_kernel, out_shape=jax.ShapeDtypeStruct((1, NFFT, c...]
where the time goes in v3:
time: 48.2 us; the launch traced here: 48.1 us
  Pallas kernels  47.4 us (98%)
  between operations  0.66 us (1%)
    pallas_call x1, Pallas kernels, per_device(): pl.pallas_call(functools.partial(kernel, (nx, ny), cells * nx * ny), out_...  46.2 us
    pallas_call x1, Pallas kernels, per_device(): pl.pallas_call(inverse_kernel, out_shape=jax.ShapeDtypeStruct((1, NFFT, c...  1.21 us

profile of v3, /device:TPU:1, one launch (start us, length us, event | category | flops | bytes accessed | tf_op | source)
XLA Modules:
  0.0 48.1 jit_solution(2889222231038353243)
XLA Ops:
  0.7 46.2 %exchange.1 = (bf16[256,1024]{1,0:T(8,128)(2,1)S(1)}, bf16[256,128]{1,0:T(8,128)(2,1)S(1)}) custom-call(s32[1]{0:T(128)S(6)} %copy.7.off_ref, s32[1,64]{1,0:T(1,128)} %bitcast.7, f32[8,16]{1,0:T(8,128)} %bitcast.6, f32[1,2048]{1,0:T(1,128)} %bitcast.5, bf16[1,320,2048]{2,1,0:T(8,128)(2,1)} %snap_hbm.1, bf16[256,2048]{1,0:T(8,128)(2,1)} %bitcast.4), custom_call_target="tpu_custom_call" | custom-call | tf_op jit(solution)/shard_map/exchange/pallas_call | solution.py:336
  46.9 1.2 %inverse.1 = bf16[1,256,2048]{2,1,0:T(8,128)(2,1)} custom-call(bf16[256,128]{1,0:T(8,128)(2,1)S(1)} %get-tuple-element.7.inv_ref, bf16[256,1024]{1,0:T(8,128)(2,1)S(1)} %get-tuple-element.8.ret_ref), custom_call_target="tpu_custom_call" | custom-call | tf_op jit(solution)/shard_map/inverse/pallas_call | solution.py:374

commit v4 on v3

--- a/solution.py
+++ b/solution.py
@@ -68,6 +68,20 @@
     me, ix, iy = lax.axis_index("blk"), lax.axis_index("sx"), lax.axis_index("sy")
     half = spec.shape[1]
 
+    stages = (
+        (first, ny, lambda d: {"sy": (iy + d) % ny}),
+        (second, nx, lambda d: {"sx": (ix + d) % nx}),
+    )
+    far_first = [
+        sorted(range(1, n), key=lambda d: abs(d - n // 2)) for _, n, _ in stages
+    ]
+    barrier = pltpu.get_barrier_semaphore()
+    greeted = [{"blk": (me + 2) % NB}] + [stages[1][2](d) for d in far_first[1]]
+    greeted += [{"blk": (me + 1) % NB}, {"blk": (me + 3) % NB}]
+    greeted += [stages[0][2](d) for d in far_first[0]]
+    for partner in greeted:
+        pl.semaphore_signal(barrier, inc=1, device_id=partner, device_id_type=MESH)
+
     loads = [
         pltpu.make_async_copy(src, dst, load_sem.at[i])
         for i, (src, dst) in enumerate(
@@ -80,20 +94,6 @@
     for load in loads:
         load.start()
 
-    barrier = pltpu.get_barrier_semaphore()
-    for d in range(1, NB):
-        pl.semaphore_signal(barrier, inc=1, device_id={"blk": (me + d) % NB}, device_id_type=MESH)
-
-    stages = (
-        (first, ny, lambda d: {"sy": (iy + d) % ny}),
-        (second, nx, lambda d: {"sx": (ix + d) % nx}),
-    )
-    greeted = NB - 1
-    for _, n, partner in stages:
-        greeted += n - 1
-        for d in range(1, n):
-            pl.semaphore_signal(barrier, inc=1, device_id=partner(d), device_id_type=MESH)
-
     loads[0].wait()
     rows = tab.shape[0]
 
@@ -136,8 +136,8 @@
             ]
             spec[pl.ds(q * RQ, RQ), pl.ds(c, TILE)] = halves_together(parts).astype(jnp.bfloat16)
 
-    def send_forward(q):
-        for d in (2, 1, 3):
+    def send_forward(q, partners=(2, 1, 3)):
+        for d in partners:
             if q:
                 forward_copy(q - 1, d).wait_send()
             forward_copy(q, d).start()
@@ -150,7 +150,7 @@
         low, high = snap[pl.ds(0, extra), cols], snap[pl.ds(NFFT, extra), cols]
         snap[pl.ds(0, extra), cols] = jnp.where(early, high, low)
     transform(0)
-    pl.semaphore_wait(barrier, greeted)
+    pl.semaphore_wait(barrier, len(greeted))
     send_forward(0)
     make_table(TQ, rows - TQ)
     for q in range(1, Q):
@@ -195,7 +195,7 @@
 
     def spread_out(q, stage):
         buffer, n, partner = stages[stage]
-        for d in sorted(range(1, n), key=lambda d: abs(d - n // 2)):
+        for d in far_first[stage]:
             pltpu.make_async_remote_copy(
                 src_ref=own.at[q, stage], dst_ref=buffer.at[q, d - 1],
                 send_sem=psend.at[q, stage], recv_sem=precv.at[q, stage],
@@ -209,6 +209,26 @@
             pltpu.make_async_copy(buffer.at[q], buffer.at[q], precv.at[q, stage]).wait()
             total += jnp.sum(buffer[q], axis=0)
         return total
+
+    slots = (0, K, LANES // 2, LANES // 2 + K)
+
+    def packed(coeff, q):
+        crossed = pltpu.roll(pltpu.roll(coeff, LANES - K, 1), J, 0)
+        combined = jnp.where(turn == 0, coeff + crossed, coeff - crossed)
+        mine = (side == 0) & (lane // (LANES // 2) == q % 2)
+        combined = jnp.where(mine, combined, 0.0)
+        message = combined
+        for i in range(1, NB):
+            message += pltpu.roll(pltpu.roll(combined, slots[i], 1), E - 2 * i, 0)
+        return message[:2]
+
+    def unpacked(total):
+        message = jnp.concatenate([total] * NB, axis=0)
+        combined = message
+        for i in range(1, NB):
+            combined = jnp.where(row // 2 == i, pltpu.roll(message, LANES - slots[i], 1), combined)
+        crossed = pltpu.roll(pltpu.roll(combined, K, 1), J, 0)
+        return jnp.where(side == 0, combined, jnp.where(turn == 0, -crossed, crossed))
 
     def project(q):
         for d in range(1, NB):
@@ -233,7 +253,7 @@
         for d in range(NB):
             sums = sum_of_four(jnp.where(diagonal(q), product[d * E : (d + 1) * E], 0.0), j)
             coeff += jnp.where(j == d, sums, 0.0)
-        own[q, 0] = coeff
+        own[q, 0] = packed(coeff, q)
         spread_out(q, 0)
 
     def pass_on(q, stage):
@@ -241,12 +261,7 @@
         spread_out(q, stage)
 
     def rebuild(q):
-        total = total_of(q, 1)
-        crossed = jnp.where(
-            side == 0, pltpu.roll(total, LANES - K, 1), pltpu.roll(total, K, 1)
-        )
-        crossed = pltpu.roll(crossed, J, 0)
-        both = jnp.where(side == turn, total + crossed, total - crossed)
+        both = unpacked(total_of(q, 1))
         scaled = gains[:, q // 2 * LANES : (q // 2 + 1) * LANES] * (both * scale)
         table = jnp.concatenate(
             [
@@ -280,8 +295,9 @@
 
     project(0)
     send_forward(2)
+    send_forward(3, (2,))
     project(1)
-    send_forward(3)
+    send_forward(3, (1, 3))
     pass_on(0, 1)
     project(2)
     pass_on(1, 1)
@@ -351,9 +367,9 @@
                 pltpu.VMEM((Q * RQ, half), bf16),
                 pltpu.VMEM((Q * RQ, half), bf16),
                 pltpu.VMEM((Q * RQ, half), bf16),
-                pltpu.VMEM((Q, 3, E, LANES), f32),
-                pltpu.VMEM((Q, max(ny - 1, 1), E, LANES), f32),
-                pltpu.VMEM((Q, max(nx - 1, 1), E, LANES), f32),
+                pltpu.VMEM((Q, 2, 2, LANES), f32),
+                pltpu.VMEM((Q, max(ny - 1, 1), 2, LANES), f32),
+                pltpu.VMEM((Q, max(nx - 1, 1), 2, LANES), f32),
                 dma((5,)), dma((Q, NB)), dma((Q, NB)), dma((Q, NB)), dma((Q, NB)),
                 dma((Q, 3)), dma((Q, 3)), dma((Q,)),
             ],

time: 48.2 us -> 47.3 us (0.981)
  Pallas kernels: 47.4 us -> 46.5 us
    pallas_call x1, Pallas kernels: 46.2 us -> 45.3 us  [per_device(): pl.pallas_call(functools.partial(kernel, (nx, ny), cells * nx * ny), out_...]
where the time goes in v4:
time: 47.3 us; the launch traced here: 47.2 us
  Pallas kernels  46.5 us (98%)
  between operations  0.66 us (1%)
    pallas_call x1, Pallas kernels, per_device(): pl.pallas_call(functools.partial(kernel, (nx, ny), cells * nx * ny), out_...  45.3 us
    pallas_call x1, Pallas kernels, per_device(): pl.pallas_call(inverse_kernel, out_shape=jax.ShapeDtypeStruct((1, NFFT, c...  1.22 us

profile of v4, /device:TPU:1, one launch (start us, length us, event | category | flops | bytes accessed | tf_op | source)
XLA Modules:
  0.0 47.2 jit_solution(4507793684278726799)
XLA Ops:
  0.7 45.3 %exchange.1 = (bf16[256,1024]{1,0:T(8,128)(2,1)S(1)}, bf16[256,128]{1,0:T(8,128)(2,1)S(1)}) custom-call(s32[1]{0:T(128)S(6)} %copy.7.off_ref, s32[1,64]{1,0:T(1,128)} %bitcast.7, f32[8,16]{1,0:T(8,128)} %bitcast.6, f32[1,2048]{1,0:T(1,128)} %bitcast.5, bf16[1,320,2048]{2,1,0:T(8,128)(2,1)} %snap_hbm.1, bf16[256,2048]{1,0:T(8,128)(2,1)} %bitcast.4), custom_call_target="tpu_custom_call" | custom-call | tf_op jit(solution)/shard_map/exchange/pallas_call | solution.py:352
  46.0 1.2 %inverse.1 = bf16[1,256,2048]{2,1,0:T(8,128)(2,1)} custom-call(bf16[256,128]{1,0:T(8,128)(2,1)S(1)} %get-tuple-element.7.inv_ref, bf16[256,1024]{1,0:T(8,128)(2,1)S(1)} %get-tuple-element.8.ret_ref), custom_call_target="tpu_custom_call" | custom-call | tf_op jit(solution)/shard_map/inverse/pallas_call | solution.py:390
